TPU v7x, 32 devices: a whole 2x2x4 slice. The times are simulated.
32 devices in a mesh: dp: 2 (over core), expert: 16 (over z, y, x).
Axes of the slice: x: 2, y: 2, z: 4, core: 2. Of those that a mesh axis runs over, the one named last changes fastest.
Arguments:
- queries: bfloat16 [2048, 2048], P('expert', 'dp'), may hold values from -60 to 60
- kv_cache: bfloat16 [256, 4, 128, 256], P('expert', 'dp'), may hold values from -4 to 4
- page_table: int32 [64, 4], P('expert'), may hold values from 0 to 15, as said below
- lengths: int32 [64], P('expert'), may hold values from 2 to 512, as said below
- residual: bfloat16 [2048, 2048], P('expert', 'dp'), may hold values from -0.59765625 to 0.59765625
- out_proj: bfloat16 [2048, 2048], P('dp'), may hold values from -0.125 to 0.125
- norm_gain: float32 [2048], replicated, may hold values from 0.5 to 1.5
- router: bfloat16 [2048, 64], replicated, may hold values from -0.09375 to 0.09375
- routes: int32 [2048, 6], P('expert'), may hold values from 0 to 63, all different within a row; in each aligned block of 64 rows (0 to 63, 64 to 127, ...) at most 12 rows name the same one
- placement: int32 [64, 2], replicated, may hold values from 0 to 127, as said below
- parity: int32 [64], replicated, may hold values 0 or 1
- slot_in: bfloat16 [2, 128, 2048, 2, 704], P('dp', 'expert'), may hold values from -0.125 to 0.125
- slot_out: bfloat16 [2, 128, 704, 2048], P('dp', 'expert'), may hold values from -0.625 to 0.625
- shared_in: bfloat16 [2048, 2, 1408], P(None, None, 'dp'), may hold values from -0.125 to 0.125
- shared_out: bfloat16 [1408, 2048], P('dp'), may hold values from -0.15625 to 0.15625
Outputs:
- layer_out: bfloat16 [2048, 2048], P('expert', 'dp')
Inputs may be any that keep to these rules, and one draw needn't show every extreme that they name: `page_table`: rows 4 j to 4 j + 3 together hold every number of 0 to 15 once. `lengths`: entry 4 j is at least 125; each aligned group of 4 entries holds one equal to 512. `routes`: the 6 entries of a row differ; in each aligned block of 64 rows no expert is named by more than 12 rows. `placement`: its 128 entries hold every slot once.
All inputs are finite; a program needn't handle non-finite values.
Results may differ from a plain program's by a relative error of at most 0.012.
Values may be sent and summed in bfloat16 or wider, within the bound.
A program may use at most 256 MiB of HBM per device.

v0:
```python
import jax
import jax.numpy as jnp
from jax import lax
from jax.sharding import PartitionSpec as P

D = 2048
HEADS = 16
KV_HEADS = 4
HEAD_DIM = 128
EXPERTS = 64
PAGE = 128
PRE = 125
BLOCK = 64
MOST = 12


masked_score = -1e30
epsilon = 1e-06


def key_owners(table, pool_pages):
    request_count = table.shape[0]
    page_width = table.shape[1]
    page_ids = jnp.arange(pool_pages, dtype=jnp.int32)
    matches = (table[None, :, :] == page_ids[:, None, None]).astype(jnp.int32)
    owners = jnp.sum(
        matches * jnp.arange(request_count, dtype=jnp.int32)[None, :, None], axis=(1, 2)
    )
    ordinal = jnp.sum(matches * jnp.arange(page_width, dtype=jnp.int32)[None, None, :], axis=(1, 2))
    offsets = jnp.arange(PAGE, dtype=jnp.int32)
    key_request = jnp.repeat(owners, PAGE)
    key_position = (ordinal[:, None] * PAGE + offsets[None, :]).reshape(-1)
    return (key_request, key_position)


def row_places(lengths, row_count):
    local = jnp.arange(row_count, dtype=jnp.int32)
    request = jnp.where(local < PRE, 0, local - PRE + 1)
    request_ids = jnp.arange(lengths.shape[0], dtype=jnp.int32)
    picked = jnp.sum(
        jnp.where(request[:, None] == request_ids[None, :], lengths[None, :], 0), axis=1
    )
    position = jnp.where(local < PRE, lengths[0] - PRE + local, picked - 1)
    return (request, position)


def attend(queries, cache, visible):
    row_count = queries.shape[0]
    pages, local_kv, page_len, _ = cache.shape
    sharing = HEADS // KV_HEADS
    keys = cache[..., :HEAD_DIM]
    values = cache[..., HEAD_DIM:]
    query_heads = queries.reshape(row_count, local_kv, sharing, HEAD_DIM)
    scores = jnp.einsum("rkgd,pkod->rkgpo", query_heads, keys, preferred_element_type=jnp.float32)
    scores = scores.reshape(row_count, local_kv, sharing, pages * page_len) * HEAD_DIM ** (-0.5)
    allowed = visible[:, None, None, :]
    scores = jnp.where(allowed, scores, masked_score)
    highest = jnp.max(scores, axis=-1)
    weights = jnp.where(allowed, jnp.exp(scores - highest[..., None]), 0.0)
    weight_sum = jnp.sum(weights, axis=-1)
    rounded = weights.astype(jnp.bfloat16).reshape(row_count, local_kv, sharing, pages, page_len)
    weighted = jnp.einsum("rkgpo,pkod->rkgd", rounded, values, preferred_element_type=jnp.float32)
    attention = (weighted / weight_sum[..., None]).astype(jnp.bfloat16)
    return attention.reshape(row_count, local_kv * sharing * HEAD_DIM)


def route_slots(routes, placement, parity, local):
    picked = (routes[:, :, None] == jnp.arange(EXPERTS, dtype=jnp.int32)[None, None, :]).astype(
        jnp.int32
    )
    flipped = jnp.sum(picked * parity[None, None, :], axis=-1)
    replica = (local[:, None] // BLOCK + flipped) % 2
    first_slot = jnp.sum(picked * placement[None, None, :, 0], axis=-1)
    second_slot = jnp.sum(picked * placement[None, None, :, 1], axis=-1)
    slot_ids = jnp.where(replica == 0, first_slot, second_slot)
    counts = jnp.sum(picked, axis=1).reshape(-1, BLOCK, EXPERTS)
    before = (jnp.cumsum(counts, axis=1) - counts).reshape(-1, EXPERTS)
    ranks = jnp.sum(picked * before[:, None, :], axis=-1)
    return (slot_ids, ranks)


def body(
    queries,
    kv_cache,
    page_table,
    lengths,
    residual,
    out_proj,
    norm_gain,
    router,
    routes,
    placement,
    parity,
    slot_in,
    slot_out,
    shared_in,
    shared_out,
):
    dp_count = lax.axis_size("dp")
    dp_place = lax.axis_index("dp")
    column_count = lax.axis_size("expert")
    row_count = queries.shape[0]
    pool_pages = kv_cache.shape[0]
    key_request, key_position = key_owners(page_table, pool_pages)
    request, position = row_places(lengths, row_count)
    visible = (key_request[None, :] == request[:, None]) & (
        key_position[None, :] <= position[:, None]
    )
    own_heads = attend(queries, kv_cache, visible)
    feature_width = D // dp_count
    projected = jnp.dot(own_heads, out_proj, preferred_element_type=jnp.float32)
    residual_full = lax.dynamic_update_slice(
        jnp.zeros_like(projected),
        residual.astype(jnp.float32),
        (jnp.zeros((), jnp.int32), dp_place * feature_width),
    )
    hidden_state = lax.psum(projected + residual_full, "dp").astype(jnp.bfloat16)
    state_float = hidden_state.astype(jnp.float32)
    mean_square = jnp.mean(state_float * state_float, axis=-1, keepdims=True)
    normed = (state_float * norm_gain[None, :] * lax.rsqrt(mean_square + epsilon)).astype(
        jnp.bfloat16
    )
    logits = jnp.dot(normed, router, preferred_element_type=jnp.float32)
    picked = routes[:, :, None] == jnp.arange(EXPERTS, dtype=jnp.int32)[None, None, :]
    chosen = jnp.sum(jnp.where(picked, logits[:, None, :], 0.0), axis=-1)
    sigmoids = jax.nn.sigmoid(chosen)
    gates = sigmoids / jnp.sum(sigmoids, axis=-1, keepdims=True)
    slots_here = slot_in.shape[1]
    half_units = slot_in.shape[4]
    slot_group = slots_here * column_count
    row_ids = jnp.arange(row_count, dtype=jnp.int32)
    slot_ids, ranks = route_slots(routes, placement, parity, row_ids)
    buffer_rows = slot_group * MOST
    targets = jnp.where(
        slot_ids // slot_group == dp_place // 2, slot_ids % slot_group * MOST + ranks, buffer_rows
    )
    source = (
        jnp.full((buffer_rows + 1,), row_count, jnp.int32)
        .at[targets.reshape(-1)]
        .set(jnp.broadcast_to(row_ids[:, None], targets.shape).reshape(-1))
    )
    gate_table = (
        jnp.zeros((buffer_rows + 1,), jnp.float32).at[targets.reshape(-1)].set(gates.reshape(-1))
    )
    source = source[:buffer_rows]
    gate_table = gate_table[:buffer_rows]
    padded = jnp.concatenate([normed, jnp.zeros((1, D), jnp.bfloat16)], axis=0)
    outgoing = padded[source].reshape(column_count, slots_here, MOST, D)
    weights_in = slot_in[0].reshape(slots_here, D, 2 * half_units)
    gate_up = jnp.einsum(
        "cumd,udh->cumh",
        lax.all_to_all(outgoing, "expert", split_axis=0, concat_axis=0, tiled=True),
        weights_in,
        preferred_element_type=jnp.float32,
    )
    hidden_units = (jax.nn.silu(gate_up[..., :half_units]) * gate_up[..., half_units:]).astype(
        jnp.bfloat16
    )
    returned = lax.all_to_all(
        jnp.einsum(
            "cumh,uhd->cumd", hidden_units, slot_out[0], preferred_element_type=jnp.float32
        ).astype(jnp.bfloat16),
        "expert",
        split_axis=0,
        concat_axis=0,
        tiled=True,
    )
    weighted_rows = returned.reshape(buffer_rows, D).astype(jnp.float32) * gate_table[:, None]
    routed = jax.ops.segment_sum(weighted_rows, source, num_segments=row_count + 1)[:row_count]
    shared_width = shared_in.shape[2]
    shared_gate_up = jnp.dot(
        normed, shared_in.reshape(D, 2 * shared_width), preferred_element_type=jnp.float32
    )
    shared_hidden = (
        jax.nn.silu(shared_gate_up[:, :shared_width]) * shared_gate_up[:, shared_width:]
    ).astype(jnp.bfloat16)
    shared_part = jnp.dot(shared_hidden, shared_out, preferred_element_type=jnp.float32)
    summed = lax.psum_scatter(
        (routed + shared_part).astype(jnp.bfloat16), "dp", scatter_dimension=1, tiled=True
    ).astype(jnp.float32)
    own_state = lax.dynamic_slice_in_dim(state_float, dp_place * feature_width, feature_width, 1)
    return (own_state + summed).astype(jnp.bfloat16)


def solution(mesh):
    in_specs = (
        P("expert", "dp"),
        P("expert", "dp", None, None),
        P("expert", None),
        P("expert"),
        P("expert", "dp"),
        P("dp", None),
        P(),
        P(),
        P("expert", None),
        P(),
        P(),
        P("dp", "expert", None, None, None),
        P("dp", "expert", None, None),
        P(None, None, "dp"),
        P("dp", None),
    )
    out_specs = P("expert", "dp")
    return jax.shard_map(body, mesh=mesh, in_specs=in_specs, out_specs=out_specs, check_vma=False)
```

profile of v0, /device:TPU:0, one launch (start us, length us, event | category | flops | bytes accessed | tf_op | source)
XLA Modules:
  0.0 483.1 jit_solution(11845070571339840299)
XLA Ops:
  10.6 3.4 scatter_custom_fusion
  16.0 3.1 fusion.55
  19.1 2.3 copy.82
  23.3 2.7 fusion.4
  26.0 2.0 fusion.8
  28.0 2.2 fusion.32
  32.0 1.9 add_dynamic-update-slice_fusion
  33.9 7.7 %all-reduce.2 = bf16[128,2048]{1,0:T(8,128)(2,1)S(1)} all-reduce(f32[128,2048]{1,0:T(8,128)} %add_dynamic-update-slice_fusion), channel_id=1, replica_groups=mesh['dp'=2,'expert'=16] {'dp'}, use_global_device_ids=true, to_apply=%region_5.6 | all-reduce | flops 262144 | bytes 1572864 | tf_op jit(solution)/shard_map/psum | solution.py:117
  43.5 7.1 %gather_fusion = bf16[1536,2048]{1,0:T(8,128)(2,1)} fusion(bf16[129,2048]{1,0:T(8,128)(2,1)S(1)} %concatenate.3, s32[2048]{0:T(1024)S(1)} %pad_clamp_fusion), kind=kCustom, calls=%fused_computation | custom fusion | bytes 12589056 | tf_op jit(solution)/shard_map/gather | solution.py:148
  50.5 10.6 %reshape.367 = bf16[16,8,12,2048]{3,2,1,0:T(8,128)(2,1)} reshape(bf16[1536,2048]{1,0:T(8,128)(2,1)} %gather_fusion) | data formatting | bytes 12582912 | tf_op jit(solution)/shard_map/reshape | solution.py:148
  61.1 7.5 %copy.63 = bf16[16,8,12,2048]{3,1,2,0:T(8,128)(2,1)S(1)} copy(bf16[16,8,12,2048]{3,2,1,0:T(8,128)(2,1)} %reshape.367) | data formatting | bytes 12582912 | tf_op jit(solution)/shard_map/reshape | solution.py:148
  68.6 147.2 %all_to_all.10 = bf16[16,8,12,2048]{3,1,2,0:T(8,128)(2,1)} all-to-all(bf16[16,8,12,2048]{3,1,2,0:T(8,128)(2,1)S(1)} %copy.63), channel_id=1, replica_groups=mesh['dp'=2,'expert'=16] {'expert'}, dimensions={0} | all-to-all | bytes 12582912 | tf_op jit(solution)/shard_map/all_to_all | solution.py:152
  215.8 27.6 %fusion.10 = f32[16,8,12,1408]{3,0,2,1:T(8,128)} fusion(bf16[8,2048,1408,1]{1,2,3,0:T(8,128)(2,1)} %bitcast.89, bf16[16,8,12,2048]{3,1,2,0:T(8,128)(2,1)} %all_to_all.10), kind=kOutput, calls=%fused_computation.17 | convolution fusion | flops 8858370048 | bytes 61079552 | tf_op jit(solution)/shard_map/cumd,udh->cumh/dot_general | solution.py:150
  243.5 15.2 %convert_bitcast_fusion = bf16[16,8,12,2048]{3,0,2,1:T(8,128)(2,1)} fusion(bf16[1,8,704,2048]{3,2,1,0:T(8,128)(2,1)} %param.27, f32[16,8,12,1408]{3,0,2,1:T(8,128)} %fusion.10), kind=kOutput, calls=%fused_computation.14 | convolution fusion | flops 4438818816 | bytes 38797312 | tf_op jit(solution)/shard_map/cumh,uhd->cumd/dot_general | solution.py:160
  258.7 8.9 %copy.66 = bf16[16,8,12,2048]{3,1,2,0:T(8,128)(2,1)} copy(bf16[16,8,12,2048]{3,0,2,1:T(8,128)(2,1)} %convert_bitcast_fusion) | data formatting | bytes 12582912 | tf_op jit(solution)/shard_map/convert_element_type | solution.py:162
  267.6 4.8 all-to-all-start.1
  274.2 3.4 scatter_custom_fusion.1
  277.6 5.5 %fusion.58 = f32[128,1408]{1,0:T(8,128)} fusion(bf16[128,2048]{1,0:T(8,128)(2,1)S(1)} %copy-done.4, bf16[2048,1408]{0,1:T(8,128)(2,1)} %bitcast.83), kind=kOutput, calls=%fused_computation.99 | convolution fusion | flops 738197504 | bytes 7012352 | tf_op jit(solution)/shard_map/dot_general | solution.py:171
  283.1 104.5 %all-to-all-done.1 = bf16[16,8,12,2048]{3,1,2,0:T(8,128)(2,1)} async-done(((bf16[16,8,12,2048]{3,1,2,0:T(8,128)(2,1)}), bf16[16,8,12,2048]{3,1,2,0:T(8,128)(2,1)}, u32[]{:S(2)}, u32[]{:S(2)}) %all-to-all-start.1) | async-done | bytes 6291488 | tf_op jit(solution)/shard_map/all_to_all | solution.py:159
  387.6 13.7 %copy.67 = f32[16,8,12,2048]{3,2,1,0:T(8,128)} copy(bf16[16,8,12,2048]{3,1,2,0:T(8,128)(2,1)} %all-to-all-done.1) | data formatting | bytes 18874368 | tf_op jit(solution)/shard_map/convert_element_type | solution.py:168
  401.4 15.8 %reshape.370 = f32[1536,2048]{1,0:T(8,128)} reshape(f32[16,8,12,2048]{3,2,1,0:T(8,128)} %copy.67) | data formatting | bytes 25165824 | tf_op jit(solution)/shard_map/convert_element_type | solution.py:168
  417.1 23.1 %scatter_custom_fusion.2 = f32[129,2048]{1,0:T(8,128)} fusion(s32[1536]{0:T(1024)S(1)} %get-tuple-element.14, f32[1536,2048]{1,0:T(8,128)} %reshape.370, f32[1536]{0:T(1024)S(1)} %bitcast.88, f32[]{:T(128)} %constant.112.clone.1), kind=kCustom, calls=%fused_computation.6 | custom fusion | flops 6291456 | bytes 13647876 | tf_op jit(solution)/shard_map/scatter-add | solution.py:169
  440.3 2.9 fusion.19
  444.3 29.9 %reduce-scatter.2.cloned.1.call-done = bf16[128,1024]{1,0:T(8,128)(2,1)} async-done(((bf16[128,2048]{1,0:T(8,128)(2,1)}), bf16[128,1024]{1,0:T(8,128)(2,1)}) %reduce-scatter.2.cloned.1.call-update) | async-done | bytes 262160 | tf_op jit(solution)/shard_map/reduce_scatter | solution.py:178
  (64 shorter events, 15.6 us)
Async XLA Ops:
  6.5 433.7 %copy-start = (bf16[704,2048]{1,0:T(8,128)(2,1)S(1)}, bf16[704,2048]{1,0:T(8,128)(2,1)}, u32[]{:S(2)}) copy-start(bf16[704,2048]{1,0:T(8,128)(2,1)} %param.29) | copy-start | bytes 8650756
  23.3 4.7 copy-start.6
  28.0 2.2 copy-start.5
  28.0 4.0 copy-start.7
  30.2 12.2 %copy-start.9 = (f32[2048]{0:T(1024)S(1)}, f32[2048]{0:T(1024)}, u32[]{:S(2)}) copy-start(f32[2048]{0:T(1024)} %param.21) | copy-start | bytes 24580
  41.6 0.8 copy-start.1
  42.6 0.8 copy-start.3
  267.5 5.0 %copy-start.4 = (bf16[128,2048]{1,0:T(8,128)(2,1)S(1)}, bf16[128,2048]{1,0:T(8,128)(2,1)}, u32[]{:S(2)}) copy-start(bf16[128,2048]{1,0:T(8,128)(2,1)} %copy-done.3) | copy-start | bytes 1572868
  267.6 6.3 %copy-start.8 = (s32[128,6]{0,1:T(8,128)S(1)}, s32[128,6]{0,1:T(8,128)}, u32[]{:S(2)}) copy-start(s32[128,6]{0,1:T(8,128)} %param.23) | copy-start | bytes 9220
  267.6 120.1 %all-to-all-start.1 = ((bf16[16,8,12,2048]{3,1,2,0:T(8,128)(2,1)}), bf16[16,8,12,2048]{3,1,2,0:T(8,128)(2,1)}, u32[]{:S(2)}, u32[]{:S(2)}) async-start(bf16[16,8,12,2048]{3,1,2,0:T(8,128)(2,1)} %copy.66), calls=%async_computation.1 | async-start | bytes 12582912 | tf_op jit(solution)/shard_map/all_to_all | solution.py:159
  272.3 201.8 %reduce-scatter.2.cloned.1.call-start = ((), (), s32[]{:S(2)}) async-start(), calls=%async_computation.3 | async-start | bytes 786432 | tf_op jit(solution)/shard_map/reduce_scatter | solution.py:178
  417.1 26.1 %copy-start.2 = (bf16[128,2048]{1,0:T(8,128)(2,1)S(1)}, bf16[128,2048]{1,0:T(8,128)(2,1)}, u32[]{:S(2)}) copy-start(bf16[128,2048]{1,0:T(8,128)(2,1)} %copy-done.1) | copy-start | bytes 1572868
Sparse Core Ops, SparseCore 0:
  443.3 30.7 reduce-scatter.1
where the time goes:
time: 491 us; the launch traced here: 483 us
  blocking collectives  155 us (32%)
  waiting for transfers between devices  134 us (27%)
  local copies, waits for them, and re-layouts  80.7 us (16%)
  matrix products  59.1 us (12%)
  other arithmetic  34.4 us (7%)
  between operations  14.6 us (3%)
  starting transfers between devices  5.01 us (1%)
    all_to_all x1, blocking collectives, body(): lax.all_to_all(outgoing, 'expert', split_axis=0, concat_axis=0, tiled=True)  147 us
    all_to_all x1, waiting for transfers between devices, body(): lax.all_to_all(jnp.einsum('cumh,uhd->cumd', hidden_units, slot_out[0], pr...  105 us
    reduce_scatter x1, waiting for transfers between devices, body(): lax.psum_scatter((routed + shared_part).astype(jnp.bfloat16), 'dp', scatt...  29.9 us
    convert_element_type x2, local copies, waits for them, and re-layouts, body(): returned.reshape(buffer_rows, D).astype(jnp.float32) * gate_table[:, None]  29.5 us
    dot_general x1, matrix products, body(): jnp.einsum('cumd,udh->cumh', lax.all_to_all(outgoing, 'expert', split_axi...  27.6 us
    scatter-add x1, other arithmetic, body(): jax.ops.segment_sum(weighted_rows, source, num_segments=row_count + 1)  23.1 us
    reshape x2, local copies, waits for them, and re-layouts, body(): outgoing = padded[source].reshape(column_count, slots_here, MOST, D)  18.1 us
    dot_general x1, matrix products, body(): jnp.einsum('cumh,uhd->cumd', hidden_units, slot_out[0], preferred_element...  15.2 us
  transfers between devices with their start and end apart: 2, of which 2 were waited for; matrix products, arithmetic and copies ran while one was open for 2% of the time, Pallas kernels for 0%

commit v1 on v0

--- a/solution.py
+++ b/solution.py
@@ -74,7 +74,17 @@
     second_slot = jnp.sum(picked * placement[None, None, :, 1], axis=-1)
     slot_ids = jnp.where(replica == 0, first_slot, second_slot)
     counts = jnp.sum(picked, axis=1).reshape(-1, BLOCK, EXPERTS)
-    before = (jnp.cumsum(counts, axis=1) - counts).reshape(-1, EXPERTS)
+    earlier = jnp.tril(jnp.ones((BLOCK, BLOCK), jnp.bfloat16), -1)
+    before = (
+        jnp.einsum(
+            "ts,bse->bte",
+            earlier,
+            counts.astype(jnp.bfloat16),
+            preferred_element_type=jnp.float32,
+        )
+        .astype(jnp.int32)
+        .reshape(-1, EXPERTS)
+    )
     ranks = jnp.sum(picked * before[:, None, :], axis=-1)
     return (slot_ids, ranks)
 

time: 491 us -> 491 us (level)
  no operation moved by 1% of the time
where the time goes in v1:
time: 491 us; the launch traced here: 483 us
  blocking collectives  155 us (32%)
  waiting for transfers between devices  134 us (27%)
  local copies, waits for them, and re-layouts  80.8 us (16%)
  matrix products  59.3 us (12%)
  other arithmetic  34.3 us (7%)
  between operations  14.6 us (3%)
  starting transfers between devices  5.01 us (1%)
    all_to_all x1, blocking collectives, body(): lax.all_to_all(outgoing, 'expert', split_axis=0, concat_axis=0, tiled=True)  147 us
    all_to_all x1, waiting for transfers between devices, body(): lax.all_to_all(jnp.einsum('cumh,uhd->cumd', hidden_units, slot_out[0], pr...  105 us
    reduce_scatter x1, waiting for transfers between devices, body(): lax.psum_scatter((routed + shared_part).astype(jnp.bfloat16), 'dp', scatt...  29.9 us
    convert_element_type x2, local copies, waits for them, and re-layouts, body(): returned.reshape(buffer_rows, D).astype(jnp.float32) * gate_table[:, None]  29.5 us
    dot_general x1, matrix products, body(): jnp.einsum('cumd,udh->cumh', lax.all_to_all(outgoing, 'expert', split_axi...  27.6 us
    scatter-add x1, other arithmetic, body(): jax.ops.segment_sum(weighted_rows, source, num_segments=row_count + 1)  23.1 us
    reshape x2, local copies, waits for them, and re-layouts, body(): outgoing = padded[source].reshape(column_count, slots_here, MOST, D)  18.1 us
    dot_general x1, matrix products, body(): jnp.einsum('cumh,uhd->cumd', hidden_units, slot_out[0], preferred_element...  15.2 us
  transfers between devices with their start and end apart: 2, of which 2 were waited for; matrix products, arithmetic and copies ran while one was open for 2% of the time, Pallas kernels for 0%

profile of v1, /device:TPU:0, one launch (start us, length us, event | category | flops | bytes accessed | tf_op | source)
XLA Modules:
  0.0 483.3 jit_solution(14522558699175085918)
XLA Ops:
  10.8 3.4 scatter_custom_fusion
  16.1 3.1 fusion.65
  19.3 2.3 copy.90
  23.5 2.7 fusion.4
  26.1 2.0 fusion.8
  28.2 2.2 fusion.33
  32.2 1.9 add_dynamic-update-slice_fusion
  34.1 7.7 %all-reduce.2 = bf16[128,2048]{1,0:T(8,128)(2,1)S(1)} all-reduce(f32[128,2048]{1,0:T(8,128)} %add_dynamic-update-slice_fusion), channel_id=1, replica_groups=mesh['dp'=2,'expert'=16] {'dp'}, use_global_device_ids=true, to_apply=%region_5.6 | all-reduce | flops 262144 | bytes 1572864 | tf_op jit(solution)/shard_map/psum | solution.py:127
  43.7 7.1 %gather_fusion = bf16[1536,2048]{1,0:T(8,128)(2,1)} fusion(bf16[129,2048]{1,0:T(8,128)(2,1)S(1)} %concatenate.3, s32[2048]{0:T(1024)S(1)} %pad_clamp_fusion), kind=kCustom, calls=%fused_computation | custom fusion | bytes 12589056 | tf_op jit(solution)/shard_map/gather | solution.py:158
  50.7 10.6 %reshape.359 = bf16[16,8,12,2048]{3,2,1,0:T(8,128)(2,1)} reshape(bf16[1536,2048]{1,0:T(8,128)(2,1)} %gather_fusion) | data formatting | bytes 12582912 | tf_op jit(solution)/shard_map/reshape | solution.py:158
  61.3 7.5 %copy.72 = bf16[16,8,12,2048]{3,1,2,0:T(8,128)(2,1)S(1)} copy(bf16[16,8,12,2048]{3,2,1,0:T(8,128)(2,1)} %reshape.359) | data formatting | bytes 12582912 | tf_op jit(solution)/shard_map/reshape | solution.py:158
  68.8 147.2 %all_to_all.10 = bf16[16,8,12,2048]{3,1,2,0:T(8,128)(2,1)} all-to-all(bf16[16,8,12,2048]{3,1,2,0:T(8,128)(2,1)S(1)} %copy.72), channel_id=1, replica_groups=mesh['dp'=2,'expert'=16] {'expert'}, dimensions={0} | all-to-all | bytes 12582912 | tf_op jit(solution)/shard_map/all_to_all | solution.py:162
  216.0 27.6 %fusion.10 = f32[16,8,12,1408]{3,0,2,1:T(8,128)} fusion(bf16[8,2048,1408,1]{1,2,3,0:T(8,128)(2,1)} %bitcast.94, bf16[16,8,12,2048]{3,1,2,0:T(8,128)(2,1)} %all_to_all.10), kind=kOutput, calls=%fused_computation.17 | convolution fusion | flops 8858370048 | bytes 61079552 | tf_op jit(solution)/shard_map/cumd,udh->cumh/dot_general | solution.py:160
  243.7 15.2 %convert_bitcast_fusion = bf16[16,8,12,2048]{3,0,2,1:T(8,128)(2,1)} fusion(bf16[1,8,704,2048]{3,2,1,0:T(8,128)(2,1)} %param.27, f32[16,8,12,1408]{3,0,2,1:T(8,128)} %fusion.10), kind=kOutput, calls=%fused_computation.14 | convolution fusion | flops 4438818816 | bytes 38797312 | tf_op jit(solution)/shard_map/cumh,uhd->cumd/dot_general | solution.py:170
  258.8 8.9 %copy.75 = bf16[16,8,12,2048]{3,1,2,0:T(8,128)(2,1)} copy(bf16[16,8,12,2048]{3,0,2,1:T(8,128)(2,1)} %convert_bitcast_fusion) | data formatting | bytes 12582912 | tf_op jit(solution)/shard_map/convert_element_type | solution.py:172
  267.7 4.8 all-to-all-start.1
  274.4 3.4 scatter_custom_fusion.1
  277.8 5.5 %fusion.68 = f32[128,1408]{1,0:T(8,128)} fusion(bf16[128,2048]{1,0:T(8,128)(2,1)S(1)} %copy-done.4, bf16[2048,1408]{0,1:T(8,128)(2,1)} %bitcast.90), kind=kOutput, calls=%fused_computation.111 | convolution fusion | flops 738197504 | bytes 7012352 | tf_op jit(solution)/shard_map/dot_general | solution.py:181
  283.3 104.5 %all-to-all-done.1 = bf16[16,8,12,2048]{3,1,2,0:T(8,128)(2,1)} async-done(((bf16[16,8,12,2048]{3,1,2,0:T(8,128)(2,1)}), bf16[16,8,12,2048]{3,1,2,0:T(8,128)(2,1)}, u32[]{:S(2)}, u32[]{:S(2)}) %all-to-all-start.1) | async-done | bytes 6291488 | tf_op jit(solution)/shard_map/all_to_all | solution.py:169
  387.8 13.7 %copy.76 = f32[16,8,12,2048]{3,2,1,0:T(8,128)} copy(bf16[16,8,12,2048]{3,1,2,0:T(8,128)(2,1)} %all-to-all-done.1) | data formatting | bytes 18874368 | tf_op jit(solution)/shard_map/convert_element_type | solution.py:178
  401.5 15.8 %reshape.362 = f32[1536,2048]{1,0:T(8,128)} reshape(f32[16,8,12,2048]{3,2,1,0:T(8,128)} %copy.76) | data formatting | bytes 25165824 | tf_op jit(solution)/shard_map/convert_element_type | solution.py:178
  417.3 23.1 %scatter_custom_fusion.2 = f32[129,2048]{1,0:T(8,128)} fusion(s32[1536]{0:T(1024)S(1)} %get-tuple-element.14, f32[1536,2048]{1,0:T(8,128)} %reshape.362, f32[1536]{0:T(1024)S(1)} %bitcast.93, f32[]{:T(128)} %constant.114.clone.1), kind=kCustom, calls=%fused_computation.6 | custom fusion | flops 6291456 | bytes 13647876 | tf_op jit(solution)/shard_map/scatter-add | solution.py:179
  440.4 2.9 fusion.19
  444.5 29.9 %reduce-scatter.2.cloned.1.call-done = bf16[128,1024]{1,0:T(8,128)(2,1)} async-done(((bf16[128,2048]{1,0:T(8,128)(2,1)}), bf16[128,1024]{1,0:T(8,128)(2,1)}) %reduce-scatter.2.cloned.1.call-update) | async-done | bytes 262160 | tf_op jit(solution)/shard_map/reduce_scatter | solution.py:188
  (66 shorter events, 15.7 us)
Async XLA Ops:
  6.5 433.9 %copy-start = (bf16[704,2048]{1,0:T(8,128)(2,1)S(1)}, bf16[704,2048]{1,0:T(8,128)(2,1)}, u32[]{:S(2)}) copy-start(bf16[704,2048]{1,0:T(8,128)(2,1)} %param.29) | copy-start | bytes 8650756
  23.5 4.7 copy-start.6
  28.2 2.2 copy-start.5
  28.2 4.0 copy-start.7
  30.4 12.2 %copy-start.9 = (f32[2048]{0:T(1024)S(1)}, f32[2048]{0:T(1024)}, u32[]{:S(2)}) copy-start(f32[2048]{0:T(1024)} %param.21) | copy-start | bytes 24580
  41.8 0.8 copy-start.1
  42.8 0.8 copy-start.3
  267.7 5.0 %copy-start.4 = (bf16[128,2048]{1,0:T(8,128)(2,1)S(1)}, bf16[128,2048]{1,0:T(8,128)(2,1)}, u32[]{:S(2)}) copy-start(bf16[128,2048]{1,0:T(8,128)(2,1)} %copy-done.3) | copy-start | bytes 1572868
  267.7 6.3 %copy-start.8 = (s32[128,6]{0,1:T(8,128)S(1)}, s32[128,6]{0,1:T(8,128)}, u32[]{:S(2)}) copy-start(s32[128,6]{0,1:T(8,128)} %param.23) | copy-start | bytes 9220
  267.7 120.1 %all-to-all-start.1 = ((bf16[16,8,12,2048]{3,1,2,0:T(8,128)(2,1)}), bf16[16,8,12,2048]{3,1,2,0:T(8,128)(2,1)}, u32[]{:S(2)}, u32[]{:S(2)}) async-start(bf16[16,8,12,2048]{3,1,2,0:T(8,128)(2,1)} %copy.75), calls=%async_computation.1 | async-start | bytes 12582912 | tf_op jit(solution)/shard_map/all_to_all | solution.py:169
  272.5 201.8 %reduce-scatter.2.cloned.1.call-start = ((), (), s32[]{:S(2)}) async-start(), calls=%async_computation.3 | async-start | bytes 786432 | tf_op jit(solution)/shard_map/reduce_scatter | solution.py:188
  417.3 26.1 %copy-start.2 = (bf16[128,2048]{1,0:T(8,128)(2,1)S(1)}, bf16[128,2048]{1,0:T(8,128)(2,1)}, u32[]{:S(2)}) copy-start(bf16[128,2048]{1,0:T(8,128)(2,1)} %copy-done.1) | copy-start | bytes 1572868
Sparse Core Ops, SparseCore 0:
  443.5 30.7 reduce-scatter.1

commit v2 on v0

--- a/solution.py
+++ b/solution.py
@@ -11,7 +11,7 @@
 PAGE = 128
 PRE = 125
 BLOCK = 64
-MOST = 12
+SEATS = 16
 
 
 masked_score = -1e30
@@ -64,19 +64,27 @@
     return attention.reshape(row_count, local_kv * sharing * HEAD_DIM)
 
 
-def route_slots(routes, placement, parity, local):
-    picked = (routes[:, :, None] == jnp.arange(EXPERTS, dtype=jnp.int32)[None, None, :]).astype(
-        jnp.int32
-    )
-    flipped = jnp.sum(picked * parity[None, None, :], axis=-1)
-    replica = (local[:, None] // BLOCK + flipped) % 2
-    first_slot = jnp.sum(picked * placement[None, None, :, 0], axis=-1)
-    second_slot = jnp.sum(picked * placement[None, None, :, 1], axis=-1)
-    slot_ids = jnp.where(replica == 0, first_slot, second_slot)
-    counts = jnp.sum(picked, axis=1).reshape(-1, BLOCK, EXPERTS)
-    before = (jnp.cumsum(counts, axis=1) - counts).reshape(-1, EXPERTS)
-    ranks = jnp.sum(picked * before[:, None, :], axis=-1)
-    return (slot_ids, ranks)
+def slot_rows(gates, placement, parity, first_slot, slots_here):
+    slot_ids = first_slot + jnp.arange(slots_here, dtype=jnp.int32)
+    held = (placement[None, :, :] == slot_ids[:, None, None]).astype(jnp.int32)
+    expert = jnp.sum(held * jnp.arange(EXPERTS, dtype=jnp.int32)[None, :, None], axis=(1, 2))
+    side = jnp.sum(held * (jnp.arange(2, dtype=jnp.int32)[None, None, :] + parity[None, :, None]), axis=(1, 2)) % 2
+    chosen = jnp.arange(EXPERTS, dtype=jnp.int32)[None, :] == expert[:, None]
+    slot_gates = jnp.sum(jnp.where(chosen, gates[:, :, :, None, :], 0.0), axis=-1)
+    named = slot_gates > 0.0
+    halves = jnp.arange(2, dtype=jnp.int32)
+    served = named & (side[None, None, None, :] == halves[None, :, None, None])
+    earlier = jnp.tril(jnp.ones((BLOCK, BLOCK), jnp.bfloat16), -1)
+    ranks = jnp.einsum(
+        "ts,cbsu->cbtu",
+        earlier,
+        served.astype(jnp.bfloat16),
+        preferred_element_type=jnp.float32,
+    ).astype(jnp.int32)
+    places = jnp.where(served, ranks, SEATS)
+    places = places.reshape(places.shape[0], 2 * BLOCK, slots_here)
+    slot_gates = slot_gates.reshape(places.shape)
+    return jnp.swapaxes(slot_gates, 1, 2), jnp.swapaxes(places, 1, 2)
 
 
 def body(
@@ -120,64 +128,62 @@
     normed = (state_float * norm_gain[None, :] * lax.rsqrt(mean_square + epsilon)).astype(
         jnp.bfloat16
     )
-    logits = jnp.dot(normed, router, preferred_element_type=jnp.float32)
-    picked = routes[:, :, None] == jnp.arange(EXPERTS, dtype=jnp.int32)[None, None, :]
-    chosen = jnp.sum(jnp.where(picked, logits[:, None, :], 0.0), axis=-1)
-    sigmoids = jax.nn.sigmoid(chosen)
-    gates = sigmoids / jnp.sum(sigmoids, axis=-1, keepdims=True)
     slots_here = slot_in.shape[1]
     half_units = slot_in.shape[4]
-    slot_group = slots_here * column_count
-    row_ids = jnp.arange(row_count, dtype=jnp.int32)
-    slot_ids, ranks = route_slots(routes, placement, parity, row_ids)
-    buffer_rows = slot_group * MOST
-    targets = jnp.where(
-        slot_ids // slot_group == dp_place // 2, slot_ids % slot_group * MOST + ranks, buffer_rows
-    )
-    source = (
-        jnp.full((buffer_rows + 1,), row_count, jnp.int32)
-        .at[targets.reshape(-1)]
-        .set(jnp.broadcast_to(row_ids[:, None], targets.shape).reshape(-1))
-    )
-    gate_table = (
-        jnp.zeros((buffer_rows + 1,), jnp.float32).at[targets.reshape(-1)].set(gates.reshape(-1))
-    )
-    source = source[:buffer_rows]
-    gate_table = gate_table[:buffer_rows]
-    padded = jnp.concatenate([normed, jnp.zeros((1, D), jnp.bfloat16)], axis=0)
-    outgoing = padded[source].reshape(column_count, slots_here, MOST, D)
-    weights_in = slot_in[0].reshape(slots_here, D, 2 * half_units)
-    gate_up = jnp.einsum(
-        "cumd,udh->cumh",
-        lax.all_to_all(outgoing, "expert", split_axis=0, concat_axis=0, tiled=True),
-        weights_in,
-        preferred_element_type=jnp.float32,
-    )
-    hidden_units = (jax.nn.silu(gate_up[..., :half_units]) * gate_up[..., half_units:]).astype(
+    own_columns = lax.dynamic_slice_in_dim(normed, dp_place * feature_width, feature_width, 1)
+    logits = jnp.dot(normed, router, preferred_element_type=jnp.float32)
+    picked = jnp.any(
+        routes[:, :, None] == jnp.arange(EXPERTS, dtype=jnp.int32)[None, None, :], axis=1
+    )
+    sigmoids = jnp.where(picked, jax.nn.sigmoid(logits), 0.0)
+    gates = sigmoids / jnp.sum(sigmoids, axis=-1, keepdims=True)
+    coarse = gates.astype(jnp.bfloat16)
+    fine = (gates - coarse.astype(jnp.float32)).astype(jnp.bfloat16)
+    sent = jnp.concatenate([own_columns, coarse, fine], axis=1)
+    arrived = lax.all_gather(sent, "expert", axis=0)
+    spread = lax.all_gather(arrived[:, :, :feature_width], "dp", axis=2, tiled=True)
+    coarse = arrived[:, :, feature_width : feature_width + EXPERTS].astype(jnp.float32)
+    fine = arrived[:, :, feature_width + EXPERTS :].astype(jnp.float32)
+    all_gates = coarse + fine
+    first_slot = lax.axis_index("expert") * slots_here
+    slot_gates, places = slot_rows(
+        all_gates.reshape(column_count, 2, BLOCK, -1), placement, parity, first_slot, slots_here
+    )
+    seat_ids = jnp.arange(SEATS, dtype=jnp.int32)
+    seated = places[:, :, None, :] == seat_ids[None, None, :, None]
+    moves = seated.astype(jnp.bfloat16).reshape(column_count, slots_here * SEATS, row_count)
+    seat_gates = jnp.sum(jnp.where(seated, slot_gates[:, :, None, :], 0.0), axis=-1)
+    seat_gates = jnp.swapaxes(seat_gates, 0, 1)
+    inputs = jnp.einsum("cst,ctd->csd", moves, spread, preferred_element_type=jnp.float32).astype(
         jnp.bfloat16
     )
-    returned = lax.all_to_all(
-        jnp.einsum(
-            "cumh,uhd->cumd", hidden_units, slot_out[0], preferred_element_type=jnp.float32
-        ).astype(jnp.bfloat16),
-        "expert",
-        split_axis=0,
-        concat_axis=0,
-        tiled=True,
-    )
-    weighted_rows = returned.reshape(buffer_rows, D).astype(jnp.float32) * gate_table[:, None]
-    routed = jax.ops.segment_sum(weighted_rows, source, num_segments=row_count + 1)[:row_count]
-    shared_width = shared_in.shape[2]
-    shared_gate_up = jnp.dot(
-        normed, shared_in.reshape(D, 2 * shared_width), preferred_element_type=jnp.float32
-    )
-    shared_hidden = (
-        jax.nn.silu(shared_gate_up[:, :shared_width]) * shared_gate_up[:, shared_width:]
-    ).astype(jnp.bfloat16)
+    inputs = jnp.swapaxes(inputs.reshape(column_count, slots_here, SEATS, D), 0, 1)
+    inputs = inputs.reshape(slots_here, column_count * SEATS, D)
+    gate_part = jnp.einsum(
+        "usd,udh->ush", inputs, slot_in[0, :, :, 0], preferred_element_type=jnp.float32
+    )
+    up_part = jnp.einsum(
+        "usd,udh->ush", inputs, slot_in[0, :, :, 1], preferred_element_type=jnp.float32
+    )
+    hidden_units = (jax.nn.silu(gate_part) * up_part).astype(jnp.bfloat16)
+    results = jnp.einsum(
+        "ush,uhd->usd", hidden_units, slot_out[0], preferred_element_type=jnp.float32
+    )
+    weighted = (results * seat_gates.reshape(slots_here, -1)[:, :, None]).astype(jnp.bfloat16)
+    weighted = jnp.swapaxes(weighted.reshape(slots_here, column_count, SEATS, D), 0, 1)
+    weighted = weighted.reshape(column_count, slots_here * SEATS, D)
+    shared_gate = jnp.dot(normed, shared_in[:, 0], preferred_element_type=jnp.float32)
+    shared_up = jnp.dot(normed, shared_in[:, 1], preferred_element_type=jnp.float32)
+    shared_hidden = (jax.nn.silu(shared_gate) * shared_up).astype(jnp.bfloat16)
     shared_part = jnp.dot(shared_hidden, shared_out, preferred_element_type=jnp.float32)
-    summed = lax.psum_scatter(
-        (routed + shared_part).astype(jnp.bfloat16), "dp", scatter_dimension=1, tiled=True
+    shared_sum = lax.psum_scatter(
+        shared_part.astype(jnp.bfloat16), "dp", scatter_dimension=1, tiled=True
     ).astype(jnp.float32)
+    partial = jnp.einsum("cst,csd->ctd", moves, weighted, preferred_element_type=jnp.float32)
+    partial = partial.astype(jnp.bfloat16).reshape(column_count * row_count, D)
+    chip = lax.psum_scatter(partial, "dp", scatter_dimension=1, tiled=True)
+    routed = lax.psum_scatter(chip, "expert", scatter_dimension=0, tiled=True)
+    summed = routed.astype(jnp.float32) + shared_sum
     own_state = lax.dynamic_slice_in_dim(state_float, dp_place * feature_width, feature_width, 1)
     return (own_state + summed).astype(jnp.bfloat16)
 

time: 491 us -> 361 us (0.74); the launches traced: 483 us -> 360 us
  blocking collectives: 155 us -> 7.19 us
  waiting for transfers between devices: 134 us -> 206 us
  local copies, waits for them, and re-layouts: 80.7 us -> 36.7 us
  matrix products: 59.1 us -> 77.9 us
  other arithmetic: 34.4 us -> 17.6 us
    all_to_all x1 -> x0, blocking collectives: 147 us -> none  [body(): lax.all_to_all(outgoing, 'expert', split_axis=0, concat_axis=0, tiled=True)]
    all_to_all x1 -> x0, waiting for transfers between devices: 105 us -> none  [body(): lax.all_to_all(jnp.einsum('cumh,uhd->cumd', hidden_units, slot_out[0], pr...]
    reduce_scatter x1 -> x3, waiting for transfers between devices: 29.9 us -> 118 us  [the longest x1 98.4 us: body(): routed = lax.psum_scatter(chip, 'expert', scatter_dimension=0, tiled=True)]
    all_gather x0 -> x2, waiting for transfers between devices: none -> 87.8 us  [the longest x1 83 us: body(): arrived = lax.all_gather(sent, 'expert', axis=0)]
    convert_element_type x3 -> x0, local copies, waits for them, and re-layouts: 38.4 us -> none  [the longest x2 29.5 us: body(): returned.reshape(buffer_rows, D).astype(jnp.float32) * gate_table[:, None]]
    scatter-add x1 -> x0, other arithmetic: 23.1 us -> none  [body(): jax.ops.segment_sum(weighted_rows, source, num_segments=row_count + 1)]
    dot_general x3 -> x6, matrix products: 48.3 us -> 65 us  [the longest x1 24.8 us: body(): jnp.einsum('ush,uhd->usd', hidden_units, slot_out[0], preferred_element_t...]
    transpose x0 -> x3, local copies, waits for them, and re-layouts: none -> 16.6 us  [the longest x1 8.31 us: body(): jnp.swapaxes(weighted.reshape(slots_here, column_count, SEATS, D), 0, 1)]
  transfers between devices with their start and end apart: 2 -> 5, of which waited for: 2 -> 5; matrix products, arithmetic and copies ran while one was open for 2% -> 6% of each run, Pallas kernels for 0% -> 0%
where the time goes in v2:
time: 361 us; the launch traced here: 360 us
  waiting for transfers between devices  206 us (57%)
  matrix products  77.9 us (22%)
  local copies, waits for them, and re-layouts  36.7 us (10%)
  other arithmetic  17.6 us (5%)
  between operations  14 us (4%)
  blocking collectives  7.19 us (2%)
    reduce_scatter x1, waiting for transfers between devices, body(): routed = lax.psum_scatter(chip, 'expert', scatter_dimension=0, tiled=True)  98.4 us
    all_gather x1, waiting for transfers between devices, body(): arrived = lax.all_gather(sent, 'expert', axis=0)  83 us
    dot_general x1, matrix products, body(): jnp.einsum('ush,uhd->usd', hidden_units, slot_out[0], preferred_element_t...  24.8 us
    dot_general x1, matrix products, body(): jnp.einsum('usd,udh->ush', inputs, slot_in[0, :, :, 1], preferred_element...  18.2 us
    reduce_scatter x1, waiting for transfers between devices, body(): lax.psum_scatter(shared_part.astype(jnp.bfloat16), 'dp', scatter_dimensio...  10.3 us
    reduce_scatter x1, waiting for transfers between devices, body(): chip = lax.psum_scatter(partial, 'dp', scatter_dimension=1, tiled=True)  9.35 us
    dot_general x1, matrix products, body(): jnp.einsum('cst,ctd->csd', moves, spread, preferred_element_type=jnp.floa...  9.01 us
    dot_general x1, matrix products, body(): jnp.einsum('cst,csd->ctd', moves, weighted, preferred_element_type=jnp.fl...  8.99 us
  transfers between devices with their start and end apart: 5, of which 5 were waited for; matrix products, arithmetic and copies ran while one was open for 6% of the time, Pallas kernels for 0%

profile of v2, /device:TPU:0, one launch (start us, length us, event | category | flops | bytes accessed | tf_op | source)
XLA Modules:
  0.0 359.8 jit_solution(13402394179359922321)
XLA Ops:
  9.5 3.1 fusion.86
  12.6 2.3 copy.96
  16.8 2.7 fusion.8
  19.5 2.0 fusion.11
  21.6 2.2 fusion.51
  25.5 1.9 add_dynamic-update-slice_fusion
  27.4 7.2 %all-reduce.1 = bf16[128,2048]{1,0:T(8,128)(2,1)S(1)} all-reduce(f32[128,2048]{1,0:T(8,128)} %add_dynamic-update-slice_fusion), channel_id=1, replica_groups=mesh['dp'=2,'expert'=16] {'dp'}, use_global_device_ids=true, to_apply=%region_5.6 | all-reduce | flops 262144 | bytes 1572864 | tf_op jit(solution)/shard_map/psum | solution.py:125
  39.2 83.0 %all-gather.6.cloned.1.call-done = bf16[2048,1152]{1,0:T(8,128)(2,1)} async-done(((bf16[128,1152]{1,0:T(8,128)(2,1)}), bf16[2048,1152]{1,0:T(8,128)(2,1)}) %all-gather.6.cloned.1.call-update) | async-done | bytes 4718608 | tf_op jit(solution)/shard_map/all_gather | solution.py:143
  122.2 4.7 %slice.42 = bf16[16,128,1024]{2,1,0:T(8,128)(2,1)} slice(bf16[16,128,1152]{2,1,0:T(8,128)(2,1)} %bitcast.129), slice={[0:16], [0:128], [0:1024]} | slice | bytes 8388608 | tf_op jit(solution)/shard_map/slice | solution.py:144
  129.1 3.3 select_reduce_fusion
  134.1 2.3 copy.95
  140.8 4.8 %all-gather.4.cloned.1.call-done = bf16[16,128,2048]{2,1,0:T(8,128)(2,1)} async-done(((bf16[16,128,1024]{2,1,0:T(8,128)(2,1)}), bf16[16,128,2048]{2,1,0:T(8,128)(2,1)}) %all-gather.4.cloned.1.call-update) | async-done | bytes 8388624 | tf_op jit(solution)/shard_map/all_gather | solution.py:144
  145.6 9.0 %convolution_convert_fusion.1 = bf16[16,128,2048]{2,1,0:T(8,128)(2,1)} fusion(pred[16,128,128]{2,1,0:T(32,128)(4,1)} %bitcast_compare_fusion, bf16[16,128,2048]{2,1,0:T(8,128)(2,1)} %all-gather.4.cloned.1.call-done), kind=kOutput, calls=%fused_computation.17 | convolution fusion | flops 1077936128 | bytes 17039360 | tf_op jit(solution)/shard_map/cst,ctd->csd/dot_general | solution.py:157
  154.6 8.3 %copy.77 = bf16[8,16,16,2048]{3,2,1,0:T(8,128)(2,1)} copy(bf16[8,16,16,2048]{3,2,0,1:T(8,128)(2,1)} %bitcast.124) | data formatting | bytes 16777216 | tf_op jit(solution)/shard_map/transpose | solution.py:160
  162.9 18.2 %fusion = f32[8,256,704]{1,2,0:T(8,128)} fusion(bf16[8,256,2048]{2,1,0:T(8,128)(2,1)} %bitcast.126, bf16[1,8,2048,2,704]{2,4,3,1,0:T(8,128)(2,1)} %param.26), kind=kOutput, calls=%fused_computation | convolution fusion | flops 5905580032 | bytes 37224448 | tf_op jit(solution)/shard_map/usd,udh->ush/dot_general | solution.py:165
  181.1 24.8 %multiply_convert_fusion = bf16[8,256,2048]{2,1,0:T(8,128)(2,1)} fusion(f32[8,256]{1,0:T(8,128)S(1)} %mul.124, bf16[1,8,704,2048]{3,2,1,0:T(8,128)(2,1)} %param.27, f32[8,256,704]{1,2,0:T(8,128)} %fusion, bf16[8,256,2048]{2,1,0:T(8,128)(2,1)} %bitcast.127, bf16[1,8,2048,2,704]{2,4,3,1,0:T(8,128)(2,1)} %param.26), kind=kOutput, calls=%fused_computation.8 | convolution fusion | flops 11828199424 | bytes 68689920 | tf_op jit(solution)/shard_map/ush,uhd->usd/dot_general | solution.py:169
  205.9 8.3 %copy.82 = bf16[16,8,16,2048]{3,2,1,0:T(8,128)(2,1)} copy(bf16[16,8,16,2048]{3,2,0,1:T(8,128)(2,1)} %bitcast.128) | data formatting | bytes 16777216 | tf_op jit(solution)/shard_map/transpose | solution.py:173
  214.2 9.0 %convolution_convert_fusion = bf16[16,128,2048]{2,1,0:T(8,128)(2,1)} fusion(pred[16,128,128]{2,1,0:T(32,128)(4,1)S(1)} %copy-done.2, bf16[16,128,2048]{2,1,0:T(8,128)(2,1)} %bitcast.123), kind=kOutput, calls=%fused_computation.16 | convolution fusion | flops 1077936128 | bytes 17039360 | tf_op jit(solution)/shard_map/cst,csd->ctd/dot_general | solution.py:182
  223.3 3.7 %fusion.18 = f32[128,704]{0,1:T(8,128)} fusion(bf16[128,2048]{1,0:T(8,128)(2,1)} %copy-done.3, bf16[2048,2,704]{0,2,1:T(8,128)(2,1)} %param.28), kind=kOutput, calls=%fused_computation.22 | convolution fusion | flops 369098752 | bytes 3768320 | tf_op jit(solution)/shard_map/dot_general | solution.py:175
  227.0 5.0 %convolution_convert_fusion.2 = bf16[128,2048]{1,0:T(8,128)(2,1)} fusion(bf16[704,2048]{1,0:T(8,128)(2,1)S(1)} %copy-done, bf16[128,2048]{1,0:T(8,128)(2,1)} %copy-done.3, bf16[2048,2,704]{0,2,1:T(8,128)(2,1)} %param.28, f32[128,704]{0,1:T(8,128)} %fusion.18), kind=kOutput, calls=%fused_computation.27 | convolution fusion | flops 739000320 | bytes 7176192 | tf_op jit(solution)/shard_map/dot_general | solution.py:178
  232.1 9.4 %reduce-scatter.4.cloned.1.call-done = bf16[2048,1024]{1,0:T(8,128)(2,1)} async-done(((bf16[2048,2048]{1,0:T(8,128)(2,1)}), bf16[2048,1024]{1,0:T(8,128)(2,1)}) %reduce-scatter.4.cloned.1.call-update) | async-done | bytes 4194320 | tf_op jit(solution)/shard_map/reduce_scatter | solution.py:184
  242.5 10.3 %reduce-scatter.8.cloned.1.call-done = bf16[128,1024]{1,0:T(8,128)(2,1)} async-done(((bf16[128,2048]{1,0:T(8,128)(2,1)}), bf16[128,1024]{1,0:T(8,128)(2,1)}) %reduce-scatter.8.cloned.1.call-update) | async-done | bytes 262160 | tf_op jit(solution)/shard_map/reduce_scatter | solution.py:179
  252.8 98.4 %reduce-scatter.6.cloned.1.call-done = bf16[128,1024]{1,0:T(8,128)(2,1)} async-done(((bf16[2048,1024]{1,0:T(8,128)(2,1)}), bf16[128,1024]{1,0:T(8,128)(2,1)}) %reduce-scatter.6.cloned.1.call-update) | async-done | bytes 262160 | tf_op jit(solution)/shard_map/reduce_scatter | solution.py:185
  351.3 2.0 add_convert_fusion
  (65 shorter events, 19.8 us)
Async XLA Ops:
  6.5 220.5 %copy-start = (bf16[704,2048]{1,0:T(8,128)(2,1)S(1)}, bf16[704,2048]{1,0:T(8,128)(2,1)}, u32[]{:S(2)}) copy-start(bf16[704,2048]{1,0:T(8,128)(2,1)} %param.29) | copy-start | bytes 8650756
  6.5 115.7 %all-gather.6.cloned.1.call-start = ((), (), s32[]{:S(2)}) async-start(), calls=%async_computation.7 | async-start | bytes 5013504 | tf_op jit(solution)/shard_map/all_gather | solution.py:143
  16.8 4.7 %copy-start.4 = (bf16[16,2,128,128]{2,3,0,1:T(8,128)(2,1)S(1)}, bf16[16,2,128,128]{2,3,0,1:T(8,128)(2,1)}, u32[]{:S(2)}) copy-start(bf16[16,2,128,128]{2,3,0,1:T(8,128)(2,1)} %copy.96) | copy-start | bytes 3145732
  21.5 2.2 copy-start.1
  21.5 4.0 %copy-start.5 = (bf16[128,1024]{1,0:T(8,128)(2,1)S(1)}, bf16[128,1024]{1,0:T(8,128)(2,1)}, u32[]{:S(2)}) copy-start(bf16[128,1024]{1,0:T(8,128)(2,1)} %param.19) | copy-start | bytes 786436
  23.7 11.1 %copy-start.6 = (f32[2048]{0:T(1024)S(1)}, f32[2048]{0:T(1024)}, u32[]{:S(2)}) copy-start(f32[2048]{0:T(1024)} %param.21) | copy-start | bytes 24580
  34.6 92.7 %copy-start.8 = (s32[64]{0:T(128)S(1)}, s32[64]{0:T(128)}, u32[]{:S(2)}) copy-start(s32[64]{0:T(128)} %param.25) | copy-start | bytes 772
  34.6 92.7 %copy-start.7 = (s32[64,2]{0,1:T(2,128)S(1)}, s32[64,2]{0,1:T(2,128)}, u32[]{:S(2)}) copy-start(s32[64,2]{0,1:T(2,128)} %param.24) | copy-start | bytes 1540
  35.0 0.9 copy-start.3
  39.2 106.5 %all-gather.4.cloned.1.call-start = ((), (), s32[]{:S(2)}) async-start(), calls=%async_computation.3 | async-start | bytes 12582912 | tf_op jit(solution)/shard_map/all_gather | solution.py:144
  127.0 114.4 %reduce-scatter.4.cloned.1.call-start = ((), (), s32[]{:S(2)}) async-start(), calls=%async_computation.4 | async-start | bytes 12582912 | tf_op jit(solution)/shard_map/reduce_scatter | solution.py:184
  205.9 8.3 %copy-start.2 = (pred[16,128,128]{2,1,0:T(32,128)(4,1)S(1)}, pred[16,128,128]{2,1,0:T(32,128)(4,1)}, u32[]{:S(2)}) copy-start(pred[16,128,128]{2,1,0:T(32,128)(4,1)} %bitcast_compare_fusion) | copy-start | bytes 786436
  223.3 29.6 %reduce-scatter.8.cloned.1.call-start = ((), (), s32[]{:S(2)}) async-start(), calls=%async_computation.6 | async-start | bytes 786432 | tf_op jit(solution)/shard_map/reduce_scatter | solution.py:179
  232.0 119.3 %reduce-scatter.6.cloned.1.call-start = ((), (), s32[]{:S(2)}) async-start(), calls=%async_computation.5 | async-start | bytes 4456448 | tf_op jit(solution)/shard_map/reduce_scatter | solution.py:185
Sparse Core Ops, SparseCore 0:
  39.3 82.8 all-gather.5
  127.1 18.4 all-gather.3
  223.4 17.9 reduce-scatter.3
  243.6 9.1 reduce-scatter.7
  255.0 96.2 reduce-scatter.5
